TPU v7x, 32 devices: a whole 2x2x4 slice. The times are simulated.
32 devices in a mesh: depth: 4 (over y, x), shots: 8 (over z, core).
Axes of the slice: x: 2, y: 2, z: 4, core: 2. Of those that a mesh axis runs over, the one named last changes fastest.
Arguments:
- adj_now: float32 [8, 64, 128, 128], P('shots', 'depth'), may hold values from -6 to 6
- adj_prev: float32 [8, 64, 128, 128], P('shots', 'depth'), may hold values from -6 to 6
- fwd_snap: bfloat16 [8, 4, 64, 128, 128], P('shots', None, 'depth'), may hold values from -6 to 6
- velocity: float32 [64, 128, 128], P('depth', 'shots'), may hold values from 1 to 2
- density: float32 [64, 128, 128], P('depth', 'shots'), may hold values from 1 to 2
- shot_count: int32 [8], P('shots'), may hold values from 1 to 12, 32 in all
- rec_x: int32 [8, 256], P('shots'), may hold values from 0 to 127
- rec_y: int32 [8, 256], P('shots'), may hold values from 0 to 127
- residual: float32 [8, 4, 256], P('shots'), may hold values from -6 to 6
Outputs:
- out_now: float32 [8, 64, 128, 128], P('shots', 'depth')
- out_prev: float32 [8, 64, 128, 128], P('shots', 'depth')
- grad_vel: float32 [64, 128, 128], P('depth', 'shots')
Inputs may be any that keep to these rules, and one draw needn't show every extreme that they name: `shot_count`: the counts sum to 32; the largest is exactly 12.
All inputs are finite; a program needn't handle non-finite values.
Results may differ from a plain program's by a relative error of at most 0.0003.
Values sent between devices are 32-bit elements; how exact they have to be, the bound alone decides.
A program may use at most 64 MiB of HBM per device.

v0:
```python
import jax
import jax.numpy as jnp
from jax import lax
from jax.sharding import PartitionSpec as P


def with_halo(shard, sides, width):
    for axis, dim in sides:
        peers, length = (lax.axis_size(axis), shard.shape[dim])
        up = [(i, (i + 1) % peers) for i in range(peers - 1)]
        down = [(j, i) for i, j in up]
        last = lax.slice_in_dim(shard, length - width, length, axis=dim)
        first = lax.slice_in_dim(shard, 0, width, axis=dim)
        before = lax.ppermute(last, axis, up)
        after = lax.ppermute(first, axis, down)
        shard = jnp.concatenate([before, shard, after], axis=dim)
    return shard


def operate(field, buoy):
    padded = jnp.pad(field, 1)
    bpad = jnp.pad(buoy, 1)
    total = jnp.zeros_like(field)
    for axis in range(3):
        center = [slice(1, -1)] * 3
        ahead = list(center)
        behind = list(center)
        ahead[axis] = slice(2, None)
        behind[axis] = slice(0, -2)
        pc, pa, pb = (padded[tuple(center)], padded[tuple(ahead)], padded[tuple(behind)])
        bc, ba, bb = (bpad[tuple(center)], bpad[tuple(ahead)], bpad[tuple(behind)])
        total = total + 0.5 * (bc + ba) * (pa - pc) - 0.5 * (bb + bc) * (pc - pb)
    return total


def source_plane(rows_x, rows_y, amounts, width_x, width_y):
    onehot_x = (rows_x[:, None] == jnp.arange(width_x, dtype=jnp.int32)[None, :]).astype(
        jnp.float32
    )
    onehot_y = (rows_y[:, None] == jnp.arange(width_y, dtype=jnp.int32)[None, :]).astype(
        jnp.float32
    )
    return jnp.dot((onehot_x * amounts[:, None]).T, onehot_y, precision=lax.Precision.HIGHEST)


def body(adj_now, adj_prev, fwd_snap, velocity, density, shot_count, rec_x, rec_y, residual):
    depth_planes = adj_now.shape[1]
    width_x = adj_now.shape[2]
    width_y = adj_now.shape[3]
    steps = fwd_snap.shape[1]
    groups = lax.axis_size("shots")
    width = 1
    vel_all, rho_all = (
        lax.all_gather(velocity, "shots", axis=1, tiled=True),
        lax.all_gather(density, "shots", axis=1, tiled=True),
    )
    packed = jnp.stack([rho_all * vel_all * vel_all, 1.0 / rho_all])
    extended = with_halo(packed, (("depth", 1),), width)
    buoy_ext = extended[1]
    first = lax.axis_index("depth") * depth_planes
    snaps = fwd_snap[0]
    rows_x = rec_x[0]
    rows_y = rec_y[0]
    image = jnp.zeros((depth_planes, width_x, width_y), jnp.float32)
    kappa_ext = extended[0, width : width + depth_planes]
    global_plane = first + jnp.arange(depth_planes, dtype=jnp.int32)
    at_receivers = (global_plane == 2).astype(jnp.float32)[:, None, None]
    current = adj_now[0]
    older = adj_prev[0]
    for step in range(steps):
        moment = steps - 1 - step
        rimmed_field = with_halo(current[None], (("depth", 1),), 1)[0]
        plane = source_plane(rows_x, rows_y, residual[0, moment], width_x, width_y)
        spread = operate(rimmed_field, buoy_ext)[1:-1]
        newer = (
            2.0 * current - older + 0.08 * kappa_ext * spread + 0.08 * at_receivers * plane[None]
        )
        image = image + snaps[moment].astype(jnp.float32) * newer
        older = current
        current = newer
    weighted = shot_count[0].astype(jnp.float32) * image
    summed = lax.psum_scatter(weighted, "shots", scatter_dimension=1, tiled=True)
    grad_vel = 2.0 * density * velocity * summed / (4.0 * groups)
    return (current[None], older[None], grad_vel)


def solution(mesh):
    in_specs = (
        P("shots", "depth", None, None),
        P("shots", "depth", None, None),
        P("shots", None, "depth", None, None),
        P("depth", "shots", None),
        P("depth", "shots", None),
        P("shots"),
        P("shots", None),
        P("shots", None),
        P("shots", None, None),
    )
    out_specs = (
        P("shots", "depth", None, None),
        P("shots", "depth", None, None),
        P("depth", "shots", None),
    )
    return jax.shard_map(body, mesh=mesh, in_specs=in_specs, out_specs=out_specs, check_vma=False)
```

profile of v0, /device:TPU:0, one launch (start us, length us, event | category | flops | bytes accessed | tf_op | source)
XLA Modules:
  0.0 153.4 jit_solution(1906381389230960286)
XLA Ops:
  7.2 0.0 all-gather.3.cloned.1.call-start
  7.2 0.7 all-gather.3.cloned.1.call-update
  7.9 0.0 all-gather.5.cloned.1.call-start
  7.9 0.7 all-gather.5.cloned.1.call-update
  8.6 0.0 reduce-scatter.2.cloned.1.call-start
  8.7 0.9 fusion.105
  9.6 4.8 %collective-permute-start.2 = (f32[1,1,128,128]{3,2,1,0:T(8,128)S(1)}, f32[1,1,128,128]{3,2,1,0:T(8,128)S(1)}, u32[]{:S(2)}, u32[]{:S(2)}) collective-permute-start(f32[1,1,128,128]{3,2,1,0:T(8,128)S(1)} %get-tuple-element.45), channel_id=1, source_target_pairs={{0,8},{8,16},{16,24},{1,9},{9,17},{17,25},{2,10},{10,18},{18,26},{... | collective-permute-start | bytes 196616 | tf_op jit(solution)/shard_map/ppermute | solution.py:14
  14.4 1.3 collective-permute-start.3
  15.7 0.8 fusion.106
  16.6 1.1 fusion.79
  17.7 0.0 collective-permute-done.2
  17.7 2.9 %collective-permute-done.3 = f32[1,1,128,128]{3,2,1,0:T(8,128)S(1)} collective-permute-done((f32[1,1,128,128]{3,2,1,0:T(8,128)S(1)}, f32[1,1,128,128]{3,2,1,0:T(8,128)S(1)}, u32[]{:S(2)}, u32[]{:S(2)}) %collective-permute-start.3) | collective-permute-done | bytes 65568 | tf_op jit(solution)/shard_map/ppermute | solution.py:15
  20.6 1.3 maximum_bitcast_fusion
  21.9 12.6 %all-gather.3.cloned.1.call-done = f32[16,128,128]{2,1,0:T(8,128)} async-done(((f32[16,16,128]{2,1,0:T(8,128)}), f32[16,128,128]{2,1,0:T(8,128)}) %all-gather.3.cloned.1.call-update) | async-done | bytes 1048592 | tf_op jit(solution)/shard_map/all_gather | solution.py:55
  34.5 23.3 %all-gather.5.cloned.1.call-done = f32[16,128,128]{2,1,0:T(8,128)} async-done(((f32[16,16,128]{2,1,0:T(8,128)}), f32[16,128,128]{2,1,0:T(8,128)}) %all-gather.5.cloned.1.call-update) | async-done | bytes 1048592 | tf_op jit(solution)/shard_map/all_gather | solution.py:54
  57.8 1.8 %multiply_multiply_fusion = (f32[16,128,128]{2,1,0:T(8,128)S(1)}, f32[1,16,128,128]{3,2,1,0:T(8,128)S(1)}) fusion(f32[16,128,128]{2,1,0:T(8,128)} %all-gather.5.cloned.1.call-done, f32[16,128,128]{2,1,0:T(8,128)} %all-gather.3.cloned.1.call-done), kind=kLoop, calls=%fused_computation.30 | loop fusion | flops 786432 | bytes 4194304 | tf_op jit(solution)/shard_map/mul | solution.py:57
  59.6 3.4 %collective-permute-start = (f32[2,1,128,128]{3,2,1,0:T(8,128)S(1)}, f32[2,1,128,128]{3,2,1,0:T(8,128)S(1)}, u32[]{:S(2)}, u32[]{:S(2)}) collective-permute-start(f32[2,1,128,128]{3,2,1,0:T(8,128)S(1)} %get-tuple-element.5), channel_id=1, source_target_pairs={{0,8},{8,16},{16,24},{1,9},{9,17},{17,25},{2,10},{10,18},{18,26},{... | collective-permute-start | bytes 393224 | tf_op jit(solution)/shard_map/ppermute | solution.py:14
  63.0 1.3 collective-permute-start.1
  64.3 1.1 fusion.12
  65.4 0.7 collective-permute-done
  66.1 4.7 %collective-permute-done.1 = f32[2,1,128,128]{3,2,1,0:T(8,128)S(1)} collective-permute-done((f32[2,1,128,128]{3,2,1,0:T(8,128)S(1)}, f32[2,1,128,128]{3,2,1,0:T(8,128)S(1)}, u32[]{:S(2)}, u32[]{:S(2)}) %collective-permute-start.1) | collective-permute-done | bytes 131104 | tf_op jit(solution)/shard_map/ppermute | solution.py:15
  70.9 0.1 fusion.20
  71.0 0.0 copy-start.1
  71.0 0.0 copy-start.3
  71.0 0.8 fusion.1
  71.8 0.4 copy-done.1
  72.2 0.3 copy-done.3
  72.5 0.0 copy-start.6
  72.5 2.0 %fusion.61 = f32[16,128,128]{2,1,0:T(8,128)S(1)} fusion(f32[18,128,128]{2,1,0:T(8,128)S(1)} %get-tuple-element.34, f32[18,128,128]{2,1,0:T(8,128)S(1)} %get-tuple-element.33, f32[18,128,128]{2,1,0:T(8,128)S(1)} %get-tuple-element.32, f32[18,128,128]{2,1,0:T(8,128)S(1)} %get-tuple-element.36, f32[18,128,128]{2,1,0:T(8,128)S(1)} %maximum_bitcast_fusion, ...), kind=kLoop, calls=%fused_computation.118 | loop fusion | flops 5767168 | bytes 17891392 | tf_op jit(solution)/shard_map/add | solution.py:76
  74.5 3.7 %collective-permute-start.4 = (f32[1,1,128,128]{3,2,1,0:T(8,128)S(1)}, f32[1,1,128,128]{3,2,1,0:T(8,128)S(1)}, u32[]{:S(2)}, u32[]{:S(2)}) collective-permute-start(f32[1,1,128,128]{3,2,1,0:T(8,128)S(1)} %get-tuple-element.41), channel_id=1, source_target_pairs={{0,8},{8,16},{16,24},{1,9},{9,17},{17,25},{2,10},{10,18},{18,26},{... | collective-permute-start | bytes 196616 | tf_op jit(solution)/shard_map/ppermute | solution.py:14
  78.2 1.3 collective-permute-start.5
  79.5 0.0 copy-done.6
  79.5 0.0 copy-done.7
  79.5 0.4 fusion.77
  79.9 0.2 collective-permute-done.4
  80.1 4.3 %collective-permute-done.5 = f32[1,1,128,128]{3,2,1,0:T(8,128)S(1)} collective-permute-done((f32[1,1,128,128]{3,2,1,0:T(8,128)S(1)}, f32[1,1,128,128]{3,2,1,0:T(8,128)S(1)}, u32[]{:S(2)}, u32[]{:S(2)}) %collective-permute-start.5) | collective-permute-done | bytes 65568 | tf_op jit(solution)/shard_map/ppermute | solution.py:15
  84.4 0.1 maximum_bitcast_fusion.1
  84.5 1.2 fusion.14
  85.7 2.1 %fusion.49 = f32[16,128,128]{2,1,0:T(8,128)S(1)} fusion(f32[18,128,128]{2,1,0:T(8,128)S(1)} %get-tuple-element.22, f32[18,128,128]{2,1,0:T(8,128)S(1)} %get-tuple-element.21, f32[18,128,128]{2,1,0:T(8,128)S(1)} %get-tuple-element.20, f32[18,128,128]{2,1,0:T(8,128)S(1)} %get-tuple-element.24, f32[18,128,128]{2,1,0:T(8,128)S(1)} %maximum_bitcast_fusion.1, ...), kind=kLoop, calls=%fused_computation.100 | loop fusion | flops 5767168 | bytes 17891392 | tf_op jit(solution)/shard_map/add | solution.py:76
  87.7 3.4 %collective-permute-start.6 = (f32[1,1,128,128]{3,2,1,0:T(8,128)S(1)}, f32[1,1,128,128]{3,2,1,0:T(8,128)S(1)}, u32[]{:S(2)}, u32[]{:S(2)}) collective-permute-start(f32[1,1,128,128]{3,2,1,0:T(8,128)S(1)} %get-tuple-element.39), channel_id=1, source_target_pairs={{0,8},{8,16},{16,24},{1,9},{9,17},{17,25},{2,10},{10,18},{18,26},{... | collective-permute-start | bytes 196616 | tf_op jit(solution)/shard_map/ppermute | solution.py:14
  91.1 1.5 collective-permute-start.7
  92.6 0.4 fusion.75
  93.0 0.0 collective-permute-done.6
  93.0 4.3 %collective-permute-done.7 = f32[1,1,128,128]{3,2,1,0:T(8,128)S(1)} collective-permute-done((f32[1,1,128,128]{3,2,1,0:T(8,128)S(1)}, f32[1,1,128,128]{3,2,1,0:T(8,128)S(1)}, u32[]{:S(2)}, u32[]{:S(2)}) %collective-permute-start.7) | collective-permute-done | bytes 65568 | tf_op jit(solution)/shard_map/ppermute | solution.py:15
  97.3 0.1 maximum_bitcast_fusion.2
  97.4 1.2 fusion.16
  98.6 2.1 %fusion.37 = f32[16,128,128]{2,1,0:T(8,128)S(1)} fusion(f32[18,128,128]{2,1,0:T(8,128)S(1)} %get-tuple-element.16, f32[18,128,128]{2,1,0:T(8,128)S(1)} %get-tuple-element.15, f32[18,128,128]{2,1,0:T(8,128)S(1)} %get-tuple-element.14, f32[18,128,128]{2,1,0:T(8,128)S(1)} %get-tuple-element.18, f32[18,128,128]{2,1,0:T(8,128)S(1)} %maximum_bitcast_fusion.2, ...), kind=kLoop, calls=%fused_computation.82 | loop fusion | flops 5767168 | bytes 17891392 | tf_op jit(solution)/shard_map/add | solution.py:76
  100.6 0.0 copy-start
  100.7 2.8 %collective-permute-start.8 = (f32[1,1,128,128]{3,2,1,0:T(8,128)S(1)}, f32[1,1,128,128]{3,2,1,0:T(8,128)S(1)}, u32[]{:S(2)}, u32[]{:S(2)}) collective-permute-start(f32[1,1,128,128]{3,2,1,0:T(8,128)S(1)} %get-tuple-element.37), channel_id=1, source_target_pairs={{0,8},{8,16},{16,24},{1,9},{9,17},{17,25},{2,10},{10,18},{18,26},{... | collective-permute-start | bytes 196616 | tf_op jit(solution)/shard_map/ppermute | solution.py:14
  103.5 1.3 collective-permute-start.9
  104.8 0.4 fusion.73
  105.8 0.0 collective-permute-done.8
  105.9 3.8 %collective-permute-done.9 = f32[1,1,128,128]{3,2,1,0:T(8,128)S(1)} collective-permute-done((f32[1,1,128,128]{3,2,1,0:T(8,128)S(1)}, f32[1,1,128,128]{3,2,1,0:T(8,128)S(1)}, u32[]{:S(2)}, u32[]{:S(2)}) %collective-permute-start.9) | collective-permute-done | bytes 65568 | tf_op jit(solution)/shard_map/ppermute | solution.py:15
  109.6 0.1 maximum_bitcast_fusion.3
  109.7 0.0 copy-start.2
  109.7 1.1 fusion.18
  110.9 0.0 copy-done
  110.9 0.5 copy-done.2
  111.3 3.4 %fusion.70 = (f32[16,128,128]{2,1,0:T(8,128)}, f32[16,128,128]{2,1,0:T(8,128)}) fusion(f32[16,128,128]{2,1,0:T(8,128)S(1)} %fusion.37, f32[16,128,128]{2,1,0:T(8,128)S(1)} %fusion.49, f32[16,128,128]{2,1,0:T(8,128)S(1)} %fusion.61, bf16[1,4,16,128,128]{4,3,2,1,0:T(8,128)(2,1)S(1)} %copy-done.2, f32[]{:T(128)} %bitcast.19, f32[128,128]{1,0:T(8,128)S(1)} %fusion.73, ...), kind=kLoop, calls=%fused_computation.133 | loop fusion | flops 8912896 | bytes 22085700 | tf_op jit(solution)/shard_map/mul | solution.py:81
  114.7 0.0 reduce-scatter.2.cloned.1.call-update
  114.7 30.6 %reduce-scatter.2.cloned.1.call-done = f32[16,16,128]{2,1,0:T(8,128)} async-done(((f32[16,128,128]{2,1,0:T(8,128)}), f32[16,16,128]{2,1,0:T(8,128)}) %reduce-scatter.2.cloned.1.call-update) | async-done | bytes 131088 | tf_op jit(solution)/shard_map/reduce_scatter | solution.py:82
  145.3 0.0 copy-done.4
  145.3 0.0 copy-done.5
  145.3 1.6 %multiply_multiply_fusion.1 = f32[16,16,128]{2,1,0:T(8,128)} fusion(f32[16,16,128]{2,1,0:T(8,128)} %reduce-scatter.2.cloned.1.call-done, f32[16,16,128]{2,1,0:T(8,128)S(1)} %copy-done.5, f32[16,16,128]{2,1,0:T(8,128)S(1)} %copy-done.4), kind=kLoop, calls=%fused_computation.145 | loop fusion | flops 131072 | bytes 524288 | tf_op jit(solution)/shard_map/div | solution.py:83
  (8 shorter events, 0.1 us)
Async XLA Ops:
  7.2 27.3 %all-gather.3.cloned.1.call-start = ((), (), s32[]{:S(2)}) async-start(), calls=%async_computation.1 | async-start | bytes 1179648 | tf_op jit(solution)/shard_map/all_gather | solution.py:55
  7.9 49.9 %all-gather.5.cloned.1.call-start = ((), (), s32[]{:S(2)}) async-start(), calls=%async_computation.2 | async-start | bytes 1179648 | tf_op jit(solution)/shard_map/all_gather | solution.py:54
  8.6 136.6 %reduce-scatter.2.cloned.1.call-start = ((), (), s32[]{:S(2)}) async-start(), calls=%async_computation.3 | async-start | bytes 1179648 | tf_op jit(solution)/shard_map/reduce_scatter | solution.py:82
  9.6 8.1 %collective-permute-start.2 = (f32[1,1,128,128]{3,2,1,0:T(8,128)S(1)}, f32[1,1,128,128]{3,2,1,0:T(8,128)S(1)}, u32[]{:S(2)}, u32[]{:S(2)}) collective-permute-start(f32[1,1,128,128]{3,2,1,0:T(8,128)S(1)} %get-tuple-element.45), channel_id=1, source_target_pairs={{0,8},{8,16},{16,24},{1,9},{9,17},{17,25},{2,10},{10,18},{18,26},{... | collective-permute-start | bytes 196616 | tf_op jit(solution)/shard_map/ppermute | solution.py:14
  14.4 6.2 %collective-permute-start.3 = (f32[1,1,128,128]{3,2,1,0:T(8,128)S(1)}, f32[1,1,128,128]{3,2,1,0:T(8,128)S(1)}, u32[]{:S(2)}, u32[]{:S(2)}) collective-permute-start(f32[1,1,128,128]{3,2,1,0:T(8,128)S(1)} %get-tuple-element.46), channel_id=1, source_target_pairs={{8,0},{16,8},{24,16},{9,1},{17,9},{25,17},{10,2},{18,10},{26,18},{... | collective-permute-start | bytes 196616 | tf_op jit(solution)/shard_map/ppermute | solution.py:15
  59.6 6.5 %collective-permute-start = (f32[2,1,128,128]{3,2,1,0:T(8,128)S(1)}, f32[2,1,128,128]{3,2,1,0:T(8,128)S(1)}, u32[]{:S(2)}, u32[]{:S(2)}) collective-permute-start(f32[2,1,128,128]{3,2,1,0:T(8,128)S(1)} %get-tuple-element.5), channel_id=1, source_target_pairs={{0,8},{8,16},{16,24},{1,9},{9,17},{17,25},{2,10},{10,18},{18,26},{... | collective-permute-start | bytes 393224 | tf_op jit(solution)/shard_map/ppermute | solution.py:14
  63.0 7.9 %collective-permute-start.1 = (f32[2,1,128,128]{3,2,1,0:T(8,128)S(1)}, f32[2,1,128,128]{3,2,1,0:T(8,128)S(1)}, u32[]{:S(2)}, u32[]{:S(2)}) collective-permute-start(f32[2,1,128,128]{3,2,1,0:T(8,128)S(1)} %get-tuple-element.6), channel_id=1, source_target_pairs={{8,0},{16,8},{24,16},{9,1},{17,9},{25,17},{10,2},{18,10},{26,18},{... | collective-permute-start | bytes 393224 | tf_op jit(solution)/shard_map/ppermute | solution.py:15
  71.0 1.2 copy-start.1
  71.0 1.5 copy-start.3
  72.5 7.0 %copy-start.6 = (s32[1,256]{1,0:T(1,128)S(1)}, s32[1,256]{1,0:T(1,128)}, u32[]{:S(2)}) copy-start(s32[1,256]{1,0:T(1,128)} %param.16) | copy-start | bytes 3076
  72.5 7.0 %copy-start.7 = (s32[1,256]{1,0:T(1,128)S(1)}, s32[1,256]{1,0:T(1,128)}, u32[]{:S(2)}) copy-start(s32[1,256]{1,0:T(1,128)} %param.15) | copy-start | bytes 3076
  74.5 5.6 %collective-permute-start.4 = (f32[1,1,128,128]{3,2,1,0:T(8,128)S(1)}, f32[1,1,128,128]{3,2,1,0:T(8,128)S(1)}, u32[]{:S(2)}, u32[]{:S(2)}) collective-permute-start(f32[1,1,128,128]{3,2,1,0:T(8,128)S(1)} %get-tuple-element.41), channel_id=1, source_target_pairs={{0,8},{8,16},{16,24},{1,9},{9,17},{17,25},{2,10},{10,18},{18,26},{... | collective-permute-start | bytes 196616 | tf_op jit(solution)/shard_map/ppermute | solution.py:14
  78.2 6.2 %collective-permute-start.5 = (f32[1,1,128,128]{3,2,1,0:T(8,128)S(1)}, f32[1,1,128,128]{3,2,1,0:T(8,128)S(1)}, u32[]{:S(2)}, u32[]{:S(2)}) collective-permute-start(f32[1,1,128,128]{3,2,1,0:T(8,128)S(1)} %get-tuple-element.42), channel_id=1, source_target_pairs={{8,0},{16,8},{24,16},{9,1},{17,9},{25,17},{10,2},{18,10},{26,18},{... | collective-permute-start | bytes 196616 | tf_op jit(solution)/shard_map/ppermute | solution.py:15
  87.7 5.3 %collective-permute-start.6 = (f32[1,1,128,128]{3,2,1,0:T(8,128)S(1)}, f32[1,1,128,128]{3,2,1,0:T(8,128)S(1)}, u32[]{:S(2)}, u32[]{:S(2)}) collective-permute-start(f32[1,1,128,128]{3,2,1,0:T(8,128)S(1)} %get-tuple-element.39), channel_id=1, source_target_pairs={{0,8},{8,16},{16,24},{1,9},{9,17},{17,25},{2,10},{10,18},{18,26},{... | collective-permute-start | bytes 196616 | tf_op jit(solution)/shard_map/ppermute | solution.py:14
  91.1 6.2 %collective-permute-start.7 = (f32[1,1,128,128]{3,2,1,0:T(8,128)S(1)}, f32[1,1,128,128]{3,2,1,0:T(8,128)S(1)}, u32[]{:S(2)}, u32[]{:S(2)}) collective-permute-start(f32[1,1,128,128]{3,2,1,0:T(8,128)S(1)} %get-tuple-element.40), channel_id=1, source_target_pairs={{8,0},{16,8},{24,16},{9,1},{17,9},{25,17},{10,2},{18,10},{26,18},{... | collective-permute-start | bytes 196616 | tf_op jit(solution)/shard_map/ppermute | solution.py:15
  100.6 10.2 %copy-start = (f32[16,128,128]{2,1,0:T(8,128)}, f32[16,128,128]{2,1,0:T(8,128)S(1)}, u32[]{:S(2)}) copy-start(f32[16,128,128]{2,1,0:T(8,128)S(1)} %fusion.37) | copy-start | bytes 3145732
  100.7 5.2 %collective-permute-start.8 = (f32[1,1,128,128]{3,2,1,0:T(8,128)S(1)}, f32[1,1,128,128]{3,2,1,0:T(8,128)S(1)}, u32[]{:S(2)}, u32[]{:S(2)}) collective-permute-start(f32[1,1,128,128]{3,2,1,0:T(8,128)S(1)} %get-tuple-element.37), channel_id=1, source_target_pairs={{0,8},{8,16},{16,24},{1,9},{9,17},{17,25},{2,10},{10,18},{18,26},{... | collective-permute-start | bytes 196616 | tf_op jit(solution)/shard_map/ppermute | solution.py:14
  103.5 6.2 %collective-permute-start.9 = (f32[1,1,128,128]{3,2,1,0:T(8,128)S(1)}, f32[1,1,128,128]{3,2,1,0:T(8,128)S(1)}, u32[]{:S(2)}, u32[]{:S(2)}) collective-permute-start(f32[1,1,128,128]{3,2,1,0:T(8,128)S(1)} %get-tuple-element.38), channel_id=1, source_target_pairs={{8,0},{16,8},{24,16},{9,1},{17,9},{25,17},{10,2},{18,10},{26,18},{... | collective-permute-start | bytes 196616 | tf_op jit(solution)/shard_map/ppermute | solution.py:15
  109.7 1.6 %copy-start.2 = (bf16[1,4,16,128,128]{4,3,2,1,0:T(8,128)(2,1)S(1)}, bf16[1,4,16,128,128]{4,3,2,1,0:T(8,128)(2,1)}, u32[]{:S(2)}) copy-start(bf16[1,4,16,128,128]{4,3,2,1,0:T(8,128)(2,1)} %param.11) | copy-start | bytes 6291460
  111.3 34.0 %copy-start.4 = (f32[16,16,128]{2,1,0:T(8,128)S(1)}, f32[16,16,128]{2,1,0:T(8,128)}, u32[]{:S(2)}) copy-start(f32[16,16,128]{2,1,0:T(8,128)} %param.13) | copy-start | bytes 393220
  111.3 34.0 %copy-start.5 = (f32[16,16,128]{2,1,0:T(8,128)S(1)}, f32[16,16,128]{2,1,0:T(8,128)}, u32[]{:S(2)}) copy-start(f32[16,16,128]{2,1,0:T(8,128)} %param.12) | copy-start | bytes 393220
Sparse Core Ops, SparseCore 0:
  9.6 24.8 all-gather.2
  36.1 21.6 all-gather.4
  114.8 30.4 reduce-scatter.1
where the time goes:
time: 154 us; the launch traced here: 153 us
  waiting for transfers between devices  88.7 us (58%)
  starting transfers between devices  24.8 us (16%)
  other arithmetic  19.8 us (13%)
  between operations  14.7 us (10%)
  local copies, waits for them, and re-layouts  2.99 us (2%)
  matrix products  2.31 us (2%)
    reduce_scatter x1, waiting for transfers between devices, body(): lax.psum_scatter(weighted, 'shots', scatter_dimension=1, tiled=True)  30.6 us
    all_gather x1, waiting for transfers between devices, body(): lax.all_gather(velocity, 'shots', axis=1, tiled=True)  23.3 us
    ppermute x5, waiting for transfers between devices, with_halo(): after = lax.ppermute(first, axis, down)  19.9 us
    ppermute x5, starting transfers between devices, with_halo(): before = lax.ppermute(last, axis, up)  18.1 us
    all_gather x1, waiting for transfers between devices, body(): lax.all_gather(density, 'shots', axis=1, tiled=True)  12.6 us
    ppermute x5, starting transfers between devices, with_halo(): after = lax.ppermute(first, axis, down)  6.64 us
    add x3, other arithmetic, body(): 2.0 * current - older + 0.08 * kappa_ext * spread  6.12 us
    sub x4, other arithmetic, operate(): total = total + 0.5 * (bc + ba) * (pa - pc) - 0.5 * (bb + bc) * (pc - pb)  4.56 us
  transfers between devices with their start and end apart: 13, of which 10 were waited for; matrix products, arithmetic and copies ran while one was open for 4% of the time, Pallas kernels for 0%

commit v1 on v0

--- a/solution.py
+++ b/solution.py
@@ -1,6 +1,9 @@
+import functools
 import jax
 import jax.numpy as jnp
 from jax import lax
+from jax.experimental import pallas as pl
+from jax.experimental.pallas import tpu as pltpu
 from jax.sharding import PartitionSpec as P
 
 
@@ -84,6 +87,356 @@
     return (current[None], older[None], grad_vel)
 
 
+MESH = pl.DeviceIdType.MESH
+
+
+def kernel(
+    depths, shots, steps,
+    now_h, prev_h, snap_h, vel_h, rho_h, count, rec_x, rec_y, res,
+    out_now_h, out_prev_h, grad,
+    fa, fb, snap, rho, vel, buoy, rho_halo, buoy_halo, halo, coef, img, plane_src,
+    pair_in, pair_sum, chain_in,
+    load_sem, own_sem, gather_send, gather_recv, edge_send, edge_recv,
+    halo_send, halo_recv, pair_send, pair_recv, chain_send, chain_recv, store_sem,
+):
+    planes, width_x, width_y = fa.shape
+    rows = rho_h.shape[1]
+    chain = shots // 2
+    d, s = lax.axis_index("depth"), lax.axis_index("shots")
+    z, c = s // 2, s % 2
+    other = 2 * z + (1 - c)
+    has_below, has_above = d > 0, d < depths - 1
+
+    loads = [
+        pltpu.make_async_copy(now_h, fa, load_sem.at[0]),
+        pltpu.make_async_copy(prev_h, fb, load_sem.at[1]),
+        pltpu.make_async_copy(snap_h, snap, load_sem.at[2]),
+    ]
+
+    def slab(ref, index):
+        return ref.at[:, pl.ds(pl.multiple_of(index * rows, 8), rows), :]
+
+    model = (rho, vel)
+    model_h = (rho_h, vel_h)
+    own = [pltpu.make_async_copy(model_h[a], slab(model[a], s), own_sem.at[a]) for a in range(2)]
+
+    barrier = pltpu.get_barrier_semaphore()
+    pl.semaphore_signal(barrier, inc=1, device_id=(d, other), device_id_type=MESH)
+    for j in range(1, chain):
+        peer = 2 * ((z + j) % chain) + c
+        pl.semaphore_signal(barrier, inc=1, device_id=(d, peer), device_id_type=MESH)
+
+    @pl.when(has_below)
+    def _():
+        pl.semaphore_signal(barrier, inc=1, device_id=(d - 1, s), device_id_type=MESH)
+
+    @pl.when(has_above)
+    def _():
+        pl.semaphore_signal(barrier, inc=1, device_id=(d + 1, s), device_id_type=MESH)
+
+    for copy in own + loads:
+        copy.start()
+    pl.semaphore_wait(barrier, chain + has_below.astype(jnp.int32) + has_above.astype(jnp.int32))
+
+    def send(a, index, way, first=False):
+        target = (2 * (z - 1) + c, 2 * (z + 1) + c, other)[way]
+        return pltpu.make_async_remote_copy(
+            src_ref=model_h[a] if first else slab(model[a], index),
+            dst_ref=slab(model[a], index),
+            send_sem=gather_send.at[a, index, way],
+            recv_sem=gather_recv.at[a, index],
+            device_id=(d, target), device_id_type=MESH,
+        )
+
+    def arrived(a, index):
+        send(a, index, 2).wait_recv()
+
+    has_left, has_right = z > 0, z < chain - 1
+    for a in range(2):
+        pl.when(has_left)(lambda a=a: send(a, s, 0, True).start())
+        pl.when(has_right)(lambda a=a: send(a, s, 1, True).start())
+    for a in range(2):
+        send(a, s, 2, True).start()
+
+    def edge(step, side, src):
+        return pltpu.make_async_remote_copy(
+            src_ref=src, dst_ref=halo.at[step, pl.ds(1 - side, 1)],
+            send_sem=halo_send.at[step, side], recv_sem=halo_recv.at[step, 1 - side],
+            device_id=(d - 1 if side == 0 else d + 1, s), device_id_type=MESH,
+        )
+
+    def edge_src(field, side):
+        return field.at[pl.ds(0 if side == 0 else planes - 1, 1)]
+
+    exists = (has_below, has_above)
+    for side in range(2):
+        pl.when(exists[side])(lambda side=side: edge(0, side, edge_src(now_h, side)).start())
+
+        @pl.when(jnp.logical_not(exists[side]))
+        def _(side=side):
+            rho_halo[side] = jnp.ones((width_x, width_y), jnp.float32)
+            for step in range(steps):
+                halo[step, side] = jnp.zeros((width_x, width_y), jnp.float32)
+
+    nrec = rec_x.shape[1]
+    spot_x = lax.broadcasted_iota(jnp.int32, (width_x, nrec), 0) == rec_x[...]
+    spot_y = (lax.broadcasted_iota(jnp.int32, (width_y, nrec), 0) == rec_y[...]).astype(jnp.float32)
+    scale = jnp.where(d == 0, 0.08, 0.0).astype(jnp.float32)
+    for t in range(steps):
+        amounts = jnp.where(spot_x, res[t : t + 1, :], 0.0)
+        plane_src[t] = scale * lax.dot_general(
+            amounts, spot_y, (((1,), (1,)), ((), ())),
+            precision=lax.Precision.HIGHEST, preferred_element_type=jnp.float32,
+        )
+
+    for k in range(1, chain):
+        for a in range(2):
+
+            @pl.when(z - k >= 0)
+            def _(a=a, k=k):
+                index = 2 * (z - k) + c
+                arrived(a, index)
+                pl.when(has_right)(lambda: send(a, index, 1).start())
+                send(a, index, 2).start()
+
+            @pl.when(z + k <= chain - 1)
+            def _(a=a, k=k):
+                index = 2 * (z + k) + c
+                arrived(a, index)
+                pl.when(has_left)(lambda: send(a, index, 0).start())
+                send(a, index, 2).start()
+
+    for copy in own:
+        copy.wait()
+    for a in range(2):
+        for j in range(chain):
+            arrived(a, 2 * j + (1 - c))
+
+    def rho_edge(side):
+        return pltpu.make_async_remote_copy(
+            src_ref=edge_src(rho, side), dst_ref=rho_halo.at[pl.ds(1 - side, 1)],
+            send_sem=edge_send.at[side], recv_sem=edge_recv.at[1 - side],
+            device_id=(d - 1 if side == 0 else d + 1, s), device_id_type=MESH,
+        )
+
+    for side in range(2):
+        pl.when(exists[side])(lambda side=side: rho_edge(side).start())
+
+    row = lax.broadcasted_iota(jnp.int32, (width_x, width_y), 0)
+    col = lax.broadcasted_iota(jnp.int32, (width_x, width_y), 1)
+
+    @pl.loop(0, planes)
+    def _(i):
+        buoy[i] = 1.0 / rho[i]
+
+    def coefficients(i, below, above):
+        b = buoy[i]
+        r, v = rho[i], vel[i]
+        k = (0.08 * 0.5) * (r * v * v)
+        kb = k * b
+        total = jnp.zeros_like(b)
+        for n, (axis, shift, size, at, last) in enumerate((
+            (0, width_x - 1, width_x, row, width_x - 1),
+            (0, 1, width_x, row, 0),
+            (1, width_y - 1, width_y, col, width_y - 1),
+            (1, 1, width_y, col, 0),
+        )):
+            outside = at == last
+            w = kb + k * jnp.where(outside, 0.0, pltpu.roll(b, shift, axis))
+            total = total + w
+            coef[n, i] = jnp.where(outside, 0.0, w)
+        for n, near in ((4, below), (5, above)):
+            w = kb + k * near
+            total = total + w
+            coef[n, i] = w
+        coef[6, i] = 2.0 - total
+
+    @pl.loop(1, planes - 1)
+    def _(i):
+        coefficients(i, buoy[i - 1], buoy[i + 1])
+
+    for side in range(2):
+        pl.when(exists[side])(lambda side=side: rho_edge(1 - side).wait_recv())
+        buoy_halo[side] = jnp.where(exists[side], 1.0 / rho_halo[side], 0.0)
+    coefficients(0, buoy_halo[0], buoy[1])
+    coefficients(planes - 1, buoy[planes - 2], buoy_halo[1])
+
+    for copy in loads:
+        copy.wait()
+
+    weight = count[0].astype(jnp.float32)
+    cur, old = fa, fb
+    for step in range(steps):
+        t = steps - 1 - step
+
+        def advance(i, below, above, source=None, cur=cur, old=old, step=step, t=t):
+            p = cur[i]
+            new = coef[6, i] * p - old[i]
+            if source is not None:
+                new = new + source
+            new = new + coef[4, i] * below + coef[5, i] * above
+            new = new + coef[0, i] * pltpu.roll(p, width_x - 1, 0)
+            new = new + coef[1, i] * pltpu.roll(p, 1, 0)
+            new = new + coef[2, i] * pltpu.roll(p, width_y - 1, 1)
+            new = new + coef[3, i] * pltpu.roll(p, 1, 1)
+            old[i] = new
+            term = snap[t, i].astype(jnp.float32) * new
+            if step > 0:
+                term = img[i] + term
+            img[i] = weight * term if step == steps - 1 else term
+
+        for side in range(2):
+            pl.when(exists[side])(
+                lambda side=side, step=step: edge(step, 1 - side, edge_src(now_h, side)).wait_recv()
+            )
+        advance(0, halo[step, 0], cur[1])
+        advance(planes - 1, cur[planes - 2], halo[step, 1])
+        if step < steps - 1:
+            for side in range(2):
+                pl.when(exists[side])(
+                    lambda side=side, step=step, old=old: edge(step + 1, side, edge_src(old, side)).start()
+                )
+        advance(1, cur[0], cur[2])
+        advance(2, cur[1], cur[3], plane_src[t])
+
+        @pl.loop(3, planes - 1)
+        def _(i, advance=advance, cur=cur):
+            advance(i, cur[i - 1], cur[i + 1])
+
+        if step < steps - 1:
+            for side in range(2):
+                pl.when(exists[side])(
+                    lambda side=side, step=step, old=old: edge(step + 1, side, edge_src(old, side)).wait_send()
+                )
+        cur, old = old, cur
+
+    def to_pair(j):
+        return pltpu.make_async_remote_copy(
+            src_ref=slab(img, 2 * j + (1 - c)), dst_ref=pair_in.at[j],
+            send_sem=pair_send.at[j], recv_sem=pair_recv.at[j],
+            device_id=(d, other), device_id_type=MESH,
+        )
+
+    def to_owner(j, slot):
+        return pltpu.make_async_remote_copy(
+            src_ref=pair_sum.at[j], dst_ref=chain_in.at[slot],
+            send_sem=chain_send.at[j], recv_sem=chain_recv.at[slot],
+            device_id=(d, 2 * j + c), device_id_type=MESH,
+        )
+
+    order = [(z + j) % chain for j in range(1, chain + 1)]
+    for j in order:
+        to_pair(j).start()
+    stores = [
+        pltpu.make_async_copy(cur, out_now_h, store_sem.at[0]),
+        pltpu.make_async_copy(old, out_prev_h, store_sem.at[1]),
+    ]
+    for copy in stores:
+        copy.start()
+    for n, j in enumerate(order):
+        to_pair(j).wait_recv()
+        at = pl.ds(pl.multiple_of((2 * j + c) * rows, 8), rows)
+        pair_sum[j] = img[:, at, :] + pair_in[j]
+        if n < chain - 1:
+            to_owner(j, z).start()
+    mine = pl.ds(pl.multiple_of(s * rows, 8), rows)
+    factor = (2.0 / (4.0 * shots)) * (rho[:, mine, :] * vel[:, mine, :])
+    total = pair_sum[z]
+    for n in range(1, chain):
+        j = (z - n + chain) % chain
+        to_owner(j, j).wait_recv()
+        total = total + chain_in[j]
+    grad[...] = factor * total
+
+    for copy in stores:
+        copy.wait()
+    for j in order:
+        to_pair(j).wait_send()
+    for j in order[:-1]:
+        to_owner(j, z).wait_send()
+    for side in range(2):
+
+        @pl.when(exists[side])
+        def _(side=side):
+            edge(0, side, edge_src(now_h, side)).wait_send()
+            rho_edge(side).wait_send()
+
+    for a in range(2):
+        pl.when(has_left)(lambda a=a: send(a, s, 0, True).wait_send())
+        pl.when(has_right)(lambda a=a: send(a, s, 1, True).wait_send())
+        send(a, s, 2, True).wait_send()
+        for k in range(1, chain):
+
+            @pl.when(z - k >= 0)
+            def _(a=a, k=k):
+                index = 2 * (z - k) + c
+                pl.when(has_right)(lambda: send(a, index, 1).wait_send())
+                send(a, index, 2).wait_send()
+
+            @pl.when(z + k <= chain - 1)
+            def _(a=a, k=k):
+                index = 2 * (z + k) + c
+                pl.when(has_left)(lambda: send(a, index, 0).wait_send())
+                send(a, index, 2).wait_send()
+
+
+def fused(adj_now, adj_prev, fwd_snap, velocity, density, shot_count, rec_x, rec_y, residual):
+    depths, shots = lax.axis_size("depth"), lax.axis_size("shots")
+    field = adj_now.shape[1:]
+    planes, width_x, width_y = field
+    steps = fwd_snap.shape[1]
+    shard = velocity.shape
+    chain = shots // 2
+    anywhere = pl.BlockSpec(memory_space=pl.ANY)
+    vmem = pl.BlockSpec(memory_space=pltpu.VMEM)
+    f32 = jnp.float32
+    dma = pltpu.SemaphoreType.DMA
+    now, prev, grad = pl.pallas_call(
+        functools.partial(kernel, depths, shots, steps),
+        out_shape=(
+            jax.ShapeDtypeStruct(field, f32),
+            jax.ShapeDtypeStruct(field, f32),
+            jax.ShapeDtypeStruct(shard, f32),
+        ),
+        in_specs=[anywhere] * 5 + [pl.BlockSpec(memory_space=pltpu.SMEM)] + [vmem] * 3,
+        out_specs=(anywhere, anywhere, vmem),
+        scratch_shapes=[
+            pltpu.VMEM(field, f32),
+            pltpu.VMEM(field, f32),
+            pltpu.VMEM((steps,) + field, fwd_snap.dtype),
+            pltpu.VMEM(field, f32),
+            pltpu.VMEM(field, f32),
+            pltpu.VMEM(field, f32),
+            pltpu.VMEM((2, width_x, width_y), f32),
+            pltpu.VMEM((2, width_x, width_y), f32),
+            pltpu.VMEM((steps, 2, width_x, width_y), f32),
+            pltpu.VMEM((7,) + field, f32),
+            pltpu.VMEM(field, f32),
+            pltpu.VMEM((steps, width_x, width_y), f32),
+            pltpu.VMEM((chain,) + shard, f32),
+            pltpu.VMEM((chain,) + shard, f32),
+            pltpu.VMEM((chain,) + shard, f32),
+            dma((3,)), dma((2,)), dma((2, shots, 3)), dma((2, shots)), dma((2,)), dma((2,)),
+            dma((steps, 2)), dma((steps, 2)), dma((chain,)), dma((chain,)), dma((chain,)), dma((chain,)),
+            dma((2,)),
+        ],
+        compiler_params=pltpu.CompilerParams(
+            collective_id=0, has_side_effects=True, vmem_limit_bytes=40 << 20
+        ),
+        name="adjoint_steps",
+    )(
+        adj_now[0], adj_prev[0], fwd_snap[0], velocity, density, shot_count, rec_x, rec_y, residual[0]
+    )
+    return now[None], prev[None], grad
+
+
+def chosen(*args):
+    planes, rows = args[3].shape[:2]
+    if rows % 8 == 0 and planes > 4 and lax.axis_size("shots") % 2 == 0:
+        return fused(*args)
+    return body(*args)
+
+
 def solution(mesh):
     in_specs = (
         P("shots", "depth", None, None),
@@ -101,4 +454,4 @@
         P("shots", "depth", None, None),
         P("depth", "shots", None),
     )
-    return jax.shard_map(body, mesh=mesh, in_specs=in_specs, out_specs=out_specs, check_vma=False)
+    return jax.shard_map(chosen, mesh=mesh, in_specs=in_specs, out_specs=out_specs, check_vma=False)

time: 154 us -> 65.1 us (0.42)
  the two profiles are of different devices: /device:TPU:0 before, /device:TPU:29 now
where the time goes in v1:
time: 65.1 us; the launch traced here: 64.8 us
  Pallas kernels  53 us (81%)
  local copies, waits for them, and re-layouts  10.5 us (16%)
  between operations  1.3 us (2%)
    pallas_call x1, Pallas kernels, fused(): pl.pallas_call(functools.partial(kernel, depths, shots, steps), out_shape...  53 us
    unnamed x19, local copies, waits for them, and re-layouts  10.5 us

profile of v1, /device:TPU:29, one launch (start us, length us, event | category | flops | bytes accessed | tf_op | source)
XLA Modules:
  0.0 64.8 jit_solution(2929833222784409627)
XLA Ops:
  1.3 0.0 copy-start
  1.3 1.6 %copy-done = bf16[1,4,16,128,128]{4,3,2,1,0:T(8,128)(2,1)S(1)} copy-done((bf16[1,4,16,128,128]{4,3,2,1,0:T(8,128)(2,1)S(1)}, bf16[1,4,16,128,128]{4,3,2,1,0:T(8,128)(2,1)}, u32[]{:S(2)}) %copy-start) | copy-done | bytes 2097176
  2.9 0.0 copy-start.1
  2.9 1.2 %copy-done.1 = f32[1,16,128,128]{3,2,1,0:T(8,128)S(1)} copy-done((f32[1,16,128,128]{3,2,1,0:T(8,128)S(1)}, f32[1,16,128,128]{3,2,1,0:T(8,128)}, u32[]{:S(2)}) %copy-start.1) | copy-done | bytes 1048600
  4.1 0.0 copy-start.2
  4.1 1.2 %copy-done.2 = f32[1,16,128,128]{3,2,1,0:T(8,128)S(1)} copy-done((f32[1,16,128,128]{3,2,1,0:T(8,128)S(1)}, f32[1,16,128,128]{3,2,1,0:T(8,128)}, u32[]{:S(2)}) %copy-start.2) | copy-done | bytes 1048600
  5.3 0.0 copy-start.3
  5.3 0.9 %copy-done.3 = f32[16,16,128]{2,1,0:T(8,128)S(1)} copy-done((f32[16,16,128]{2,1,0:T(8,128)S(1)}, f32[16,16,128]{2,1,0:T(8,128)}, u32[]{:S(2)}) %copy-start.3) | copy-done | bytes 131096
  6.2 0.0 copy-start.4
  6.2 0.9 %copy-done.4 = f32[16,16,128]{2,1,0:T(8,128)S(1)} copy-done((f32[16,16,128]{2,1,0:T(8,128)S(1)}, f32[16,16,128]{2,1,0:T(8,128)}, u32[]{:S(2)}) %copy-start.4) | copy-done | bytes 131096
  7.1 0.0 copy-start.5
  7.1 0.7 %copy-done.5 = f32[1,4,256]{2,1,0:T(4,128)S(1)} copy-done((f32[1,4,256]{2,1,0:T(4,128)S(1)}, f32[1,4,256]{2,1,0:T(4,128)}, u32[]{:S(2)}) %copy-start.5) | copy-done | bytes 4120
  7.8 0.0 copy-start.6
  7.8 0.7 %copy-done.6 = s32[1,256]{1,0:T(1,128)S(1)} copy-done((s32[1,256]{1,0:T(1,128)S(1)}, s32[1,256]{1,0:T(1,128)}, u32[]{:S(2)}) %copy-start.6) | copy-done | bytes 1048
  8.5 0.0 copy-start.7
  8.5 0.7 %copy-done.7 = s32[1,256]{1,0:T(1,128)S(1)} copy-done((s32[1,256]{1,0:T(1,128)S(1)}, s32[1,256]{1,0:T(1,128)}, u32[]{:S(2)}) %copy-start.7) | copy-done | bytes 1048
  9.2 53.0 %adjoint_steps.1 = (f32[16,128,128]{2,1,0:T(8,128)S(1)}, f32[16,128,128]{2,1,0:T(8,128)S(1)}, f32[16,16,128]{2,1,0:T(8,128)S(1)}) custom-call(f32[16,128,128]{2,1,0:T(8,128)S(1)} %bitcast.7, f32[16,128,128]{2,1,0:T(8,128)S(1)} %bitcast.8, bf16[4,16,128,128]{3,2,1,0:T(8,128)(2,1)S(1)} %bitcast.6, f32[16,16,128]{2,1,0:T(8,128)S(1)} %copy-done.3, ...), custom_call_target="tpu_custom_call" | custom-call | tf_op jit(solution)/shard_map/adjoint_steps/pallas_call | solution.py:394
  62.2 1.0 %copy.16 = f32[1,16,128,128]{3,2,1,0:T(8,128)} copy(f32[1,16,128,128]{3,2,1,0:T(8,128)S(1)} %bitcast.10) | data formatting | bytes 2097152
  63.2 1.0 %copy.17 = f32[1,16,128,128]{3,2,1,0:T(8,128)} copy(f32[1,16,128,128]{3,2,1,0:T(8,128)S(1)} %bitcast.9) | data formatting | bytes 2097152
  64.1 0.7 %copy.18 = f32[16,16,128]{2,1,0:T(8,128)} copy(f32[16,16,128]{2,1,0:T(8,128)S(1)} %get-tuple-element.14) | data formatting | bytes 262144
Async XLA Ops:
  1.3 1.6 %copy-start = (bf16[1,4,16,128,128]{4,3,2,1,0:T(8,128)(2,1)S(1)}, bf16[1,4,16,128,128]{4,3,2,1,0:T(8,128)(2,1)}, u32[]{:S(2)}) copy-start(bf16[1,4,16,128,128]{4,3,2,1,0:T(8,128)(2,1)} %param.11) | copy-start | bytes 6291460
  2.9 1.2 %copy-start.1 = (f32[1,16,128,128]{3,2,1,0:T(8,128)S(1)}, f32[1,16,128,128]{3,2,1,0:T(8,128)}, u32[]{:S(2)}) copy-start(f32[1,16,128,128]{3,2,1,0:T(8,128)} %param.9) | copy-start | bytes 3145732
  4.1 1.2 %copy-start.2 = (f32[1,16,128,128]{3,2,1,0:T(8,128)S(1)}, f32[1,16,128,128]{3,2,1,0:T(8,128)}, u32[]{:S(2)}) copy-start(f32[1,16,128,128]{3,2,1,0:T(8,128)} %param.10) | copy-start | bytes 3145732
  5.3 0.9 %copy-start.3 = (f32[16,16,128]{2,1,0:T(8,128)S(1)}, f32[16,16,128]{2,1,0:T(8,128)}, u32[]{:S(2)}) copy-start(f32[16,16,128]{2,1,0:T(8,128)} %vel_h.1) | copy-start | bytes 393220
  6.2 0.9 %copy-start.4 = (f32[16,16,128]{2,1,0:T(8,128)S(1)}, f32[16,16,128]{2,1,0:T(8,128)}, u32[]{:S(2)}) copy-start(f32[16,16,128]{2,1,0:T(8,128)} %rho_h.1) | copy-start | bytes 393220
  7.1 0.7 %copy-start.5 = (f32[1,4,256]{2,1,0:T(4,128)S(1)}, f32[1,4,256]{2,1,0:T(4,128)}, u32[]{:S(2)}) copy-start(f32[1,4,256]{2,1,0:T(4,128)} %param.17) | copy-start | bytes 12292
  7.8 0.7 %copy-start.6 = (s32[1,256]{1,0:T(1,128)S(1)}, s32[1,256]{1,0:T(1,128)}, u32[]{:S(2)}) copy-start(s32[1,256]{1,0:T(1,128)} %rec_x.1) | copy-start | bytes 3076
  8.5 0.7 %copy-start.7 = (s32[1,256]{1,0:T(1,128)S(1)}, s32[1,256]{1,0:T(1,128)}, u32[]{:S(2)}) copy-start(s32[1,256]{1,0:T(1,128)} %rec_y.1) | copy-start | bytes 3076

commit v2 on v1

--- a/solution.py
+++ b/solution.py
@@ -92,12 +92,12 @@
 
 def kernel(
     depths, shots, steps,
-    now_h, prev_h, snap_h, vel_h, rho_h, count, rec_x, rec_y, res,
+    now_h, prev_h, snap_h, vel_h, rho_h, count, rec_x_h, rec_y_h, res_h,
     out_now_h, out_prev_h, grad,
-    fa, fb, snap, rho, vel, buoy, rho_halo, buoy_halo, halo, coef, img, plane_src,
+    rec_x, rec_y, res, fa, fb, snap, rho, vel, buoy, rho_halo, buoy_halo, halo, coef, img, plane_src,
     pair_in, pair_sum, chain_in,
     load_sem, own_sem, gather_send, gather_recv, edge_send, edge_recv,
-    halo_send, halo_recv, pair_send, pair_recv, chain_send, chain_recv, store_sem,
+    halo_send, halo_recv, pair_send, pair_recv, chain_send, chain_recv, store_sem, small_sem,
 ):
     planes, width_x, width_y = fa.shape
     rows = rho_h.shape[1]
@@ -112,6 +112,10 @@
         pltpu.make_async_copy(prev_h, fb, load_sem.at[1]),
         pltpu.make_async_copy(snap_h, snap, load_sem.at[2]),
     ]
+    small = [
+        pltpu.make_async_copy(a, b, small_sem.at[n])
+        for n, (a, b) in enumerate(((rec_x_h, rec_x), (rec_y_h, rec_y), (res_h, res)))
+    ]
 
     def slab(ref, index):
         return ref.at[:, pl.ds(pl.multiple_of(index * rows, 8), rows), :]
@@ -134,7 +138,7 @@
     def _():
         pl.semaphore_signal(barrier, inc=1, device_id=(d + 1, s), device_id_type=MESH)
 
-    for copy in own + loads:
+    for copy in own + small + loads:
         copy.start()
     pl.semaphore_wait(barrier, chain + has_below.astype(jnp.int32) + has_above.astype(jnp.int32))
 
@@ -178,6 +182,8 @@
             for step in range(steps):
                 halo[step, side] = jnp.zeros((width_x, width_y), jnp.float32)
 
+    for copy in small:
+        copy.wait()
     nrec = rec_x.shape[1]
     spot_x = lax.broadcasted_iota(jnp.int32, (width_x, nrec), 0) == rec_x[...]
     spot_y = (lax.broadcasted_iota(jnp.int32, (width_y, nrec), 0) == rec_y[...]).astype(jnp.float32)
@@ -398,9 +404,12 @@
             jax.ShapeDtypeStruct(field, f32),
             jax.ShapeDtypeStruct(shard, f32),
         ),
-        in_specs=[anywhere] * 5 + [pl.BlockSpec(memory_space=pltpu.SMEM)] + [vmem] * 3,
+        in_specs=[anywhere] * 5 + [pl.BlockSpec(memory_space=pltpu.SMEM)] + [anywhere] * 3,
         out_specs=(anywhere, anywhere, vmem),
         scratch_shapes=[
+            pltpu.VMEM(rec_x.shape, rec_x.dtype),
+            pltpu.VMEM(rec_y.shape, rec_y.dtype),
+            pltpu.VMEM(residual.shape[1:], f32),
             pltpu.VMEM(field, f32),
             pltpu.VMEM(field, f32),
             pltpu.VMEM((steps,) + field, fwd_snap.dtype),
@@ -418,10 +427,10 @@
             pltpu.VMEM((chain,) + shard, f32),
             dma((3,)), dma((2,)), dma((2, shots, 3)), dma((2, shots)), dma((2,)), dma((2,)),
             dma((steps, 2)), dma((steps, 2)), dma((chain,)), dma((chain,)), dma((chain,)), dma((chain,)),
-            dma((2,)),
+            dma((2,)), dma((3,)),
         ],
         compiler_params=pltpu.CompilerParams(
-            collective_id=0, has_side_effects=True, vmem_limit_bytes=40 << 20
+            collective_id=0, has_side_effects=True, vmem_limit_bytes=60 << 20
         ),
         name="adjoint_steps",
     )(

time: 65.1 us -> 59.4 us (0.912)
  local copies, waits for them, and re-layouts: 10.5 us -> 4.02 us
  Pallas kernels: 53 us -> 53.9 us
    unnamed x19 -> x7, local copies, waits for them, and re-layouts: 10.5 us -> 4.02 us
    pallas_call x1, Pallas kernels: 53 us -> 53.9 us  [fused(): pl.pallas_call(functools.partial(kernel, depths, shots, steps), out_shape...]
where the time goes in v2:
time: 59.4 us; the launch traced here: 59.2 us
  Pallas kernels  53.9 us (91%)
  local copies, waits for them, and re-layouts  4.02 us (7%)
  between operations  1.3 us (2%)
    pallas_call x1, Pallas kernels, fused(): pl.pallas_call(functools.partial(kernel, depths, shots, steps), out_shape...  53.9 us
    unnamed x7, local copies, waits for them, and re-layouts  4.02 us

profile of v2, /device:TPU:29, one launch (start us, length us, event | category | flops | bytes accessed | tf_op | source)
XLA Modules:
  0.0 59.2 jit_solution(2650931368466792917)
XLA Ops:
  1.3 53.9 %adjoint_steps.1 = (f32[16,128,128]{2,1,0:T(8,128)}, f32[16,128,128]{2,1,0:T(8,128)}, f32[16,16,128]{2,1,0:T(8,128)}) custom-call(f32[16,128,128]{2,1,0:T(8,128)} %bitcast.7, f32[16,128,128]{2,1,0:T(8,128)} %bitcast.8, bf16[4,16,128,128]{3,2,1,0:T(8,128)(2,1)} %bitcast.6, f32[16,16,128]{2,1,0:T(8,128)} %vel_h.1, f32[16,16,128]{2,1,0:T(8,128)} %rho_h.1, ...), custom_call_target="tpu_custom_call" | custom-call | tf_op jit(solution)/shard_map/adjoint_steps/pallas_call | solution.py:400
  55.2 0.0 copy-start
  55.2 0.0 copy-start.1
  55.2 2.4 %copy.16 = f32[1,16,128,128]{3,2,1,0:T(8,128)} copy(f32[1,16,128,128]{3,2,1,0:T(8,128)} %bitcast.10) | data formatting | bytes 2097152
  57.6 0.0 copy-done
  57.6 1.0 %copy.17 = f32[1,16,128,128]{3,2,1,0:T(8,128)} copy(f32[1,16,128,128]{3,2,1,0:T(8,128)S(1)} %bitcast.9) | data formatting | bytes 2097152
  58.6 0.0 copy-done.1
  58.6 0.7 %copy.18 = f32[16,16,128]{2,1,0:T(8,128)} copy(f32[16,16,128]{2,1,0:T(8,128)S(1)} %copy-done.1) | data formatting | bytes 262144
Async XLA Ops:
  55.2 2.4 %copy-start = (f32[16,128,128]{2,1,0:T(8,128)S(1)}, f32[16,128,128]{2,1,0:T(8,128)}, u32[]{:S(2)}) copy-start(f32[16,128,128]{2,1,0:T(8,128)} %get-tuple-element.7) | copy-start | bytes 3145732
  55.2 3.4 %copy-start.1 = (f32[16,16,128]{2,1,0:T(8,128)S(1)}, f32[16,16,128]{2,1,0:T(8,128)}, u32[]{:S(2)}) copy-start(f32[16,16,128]{2,1,0:T(8,128)} %get-tuple-element.14) | copy-start | bytes 393220

commit v3 on v2

--- a/solution.py
+++ b/solution.py
@@ -295,10 +295,11 @@
             pl.when(exists[side])(
                 lambda side=side, step=step: edge(step, 1 - side, edge_src(now_h, side)).wait_recv()
             )
-        advance(0, halo[step, 0], cur[1])
-        advance(planes - 1, cur[planes - 2], halo[step, 1])
-        if step < steps - 1:
-            for side in range(2):
+            if side == 0:
+                advance(0, halo[step, 0], cur[1])
+            else:
+                advance(planes - 1, cur[planes - 2], halo[step, 1])
+            if step < steps - 1:
                 pl.when(exists[side])(
                     lambda side=side, step=step, old=old: edge(step + 1, side, edge_src(old, side)).start()
                 )

time: 59.4 us -> 58.6 us (0.987)
  Pallas kernels: 53.9 us -> 53.1 us
    pallas_call x1, Pallas kernels: 53.9 us -> 53.1 us  [fused(): pl.pallas_call(functools.partial(kernel, depths, shots, steps), out_shape...]
where the time goes in v3:
time: 58.6 us; the launch traced here: 58.5 us
  Pallas kernels  53.1 us (91%)
  local copies, waits for them, and re-layouts  4.02 us (7%)
  between operations  1.3 us (2%)
    pallas_call x1, Pallas kernels, fused(): pl.pallas_call(functools.partial(kernel, depths, shots, steps), out_shape...  53.1 us
    unnamed x7, local copies, waits for them, and re-layouts  4.02 us

profile of v3, /device:TPU:29, one launch (start us, length us, event | category | flops | bytes accessed | tf_op | source)
XLA Modules:
  0.0 58.5 jit_solution(17524867968708009234)
XLA Ops:
  1.3 53.1 %adjoint_steps.1 = (f32[16,128,128]{2,1,0:T(8,128)}, f32[16,128,128]{2,1,0:T(8,128)}, f32[16,16,128]{2,1,0:T(8,128)}) custom-call(f32[16,128,128]{2,1,0:T(8,128)} %bitcast.7, f32[16,128,128]{2,1,0:T(8,128)} %bitcast.8, bf16[4,16,128,128]{3,2,1,0:T(8,128)(2,1)} %bitcast.6, f32[16,16,128]{2,1,0:T(8,128)} %vel_h.1, f32[16,16,128]{2,1,0:T(8,128)} %rho_h.1, ...), custom_call_target="tpu_custom_call" | custom-call | tf_op jit(solution)/shard_map/adjoint_steps/pallas_call | solution.py:401
  54.4 0.0 copy-start
  54.4 0.0 copy-start.1
  54.4 2.4 %copy.16 = f32[1,16,128,128]{3,2,1,0:T(8,128)} copy(f32[1,16,128,128]{3,2,1,0:T(8,128)} %bitcast.10) | data formatting | bytes 2097152
  56.8 0.0 copy-done
  56.8 1.0 %copy.17 = f32[1,16,128,128]{3,2,1,0:T(8,128)} copy(f32[1,16,128,128]{3,2,1,0:T(8,128)S(1)} %bitcast.9) | data formatting | bytes 2097152
  57.8 0.0 copy-done.1
  57.8 0.7 %copy.18 = f32[16,16,128]{2,1,0:T(8,128)} copy(f32[16,16,128]{2,1,0:T(8,128)S(1)} %copy-done.1) | data formatting | bytes 262144
Async XLA Ops:
  54.4 2.4 %copy-start = (f32[16,128,128]{2,1,0:T(8,128)S(1)}, f32[16,128,128]{2,1,0:T(8,128)}, u32[]{:S(2)}) copy-start(f32[16,128,128]{2,1,0:T(8,128)} %get-tuple-element.7) | copy-start | bytes 3145732
  54.4 3.4 %copy-start.1 = (f32[16,16,128]{2,1,0:T(8,128)S(1)}, f32[16,16,128]{2,1,0:T(8,128)}, u32[]{:S(2)}) copy-start(f32[16,16,128]{2,1,0:T(8,128)} %get-tuple-element.14) | copy-start | bytes 393220
